TPU v7x, 32 devices: a whole 2x2x4 slice. The times are simulated.
32 devices in a mesh: row: 4 (over y, core), col: 8 (over z, x).
Axes of the slice: x: 2, y: 2, z: 4, core: 2. Of those that a mesh axis runs over, the one named last changes fastest.
Arguments:
- transition: bfloat16 [32768, 32768], P('row', 'col'), may hold values from 1.5258789e-06 to 0.0024414062, as said below
- emission: bfloat16 [96, 32768], P(None, 'col'), may hold values from 0.0099487305 to 1
- token_ids: int32 [2, 192], replicated, may hold values from 0 to 95
- forward: bfloat16 [2, 192, 32768], P(None, 'col', 'row'), may hold values from 3.0517578e-06 to 0.0008239746, as said below
- backward_last: float32 [192, 32768], P('row', 'col'), may hold values from 0.1 to 10
Outputs:
- backward: float32 [2, 192, 32768], P(None, 'col', 'row')
- counts: float32 [32768, 1024], P('row', 'col')
Inputs may be any that keep to these rules, and one draw needn't show every extreme that they name: Positive transition weights. Positive forward weights.
All inputs are finite; a program needn't handle non-finite values.
Results may differ from a plain program's by a relative error of at most 0.00048.
Values may be sent and summed in bfloat16 or wider, within the bound.
A program may use at most 192 MiB of HBM per device.

v0:
```python
import jax
import jax.numpy as jnp
from jax import lax
from jax.sharding import PartitionSpec as P

H = 32768
N = 192
DW = 128


def spread(value, axis, source):
    kept = jnp.where(lax.axis_index(axis) == source, value, 0).astype(value.dtype)
    return lax.psum(kept, axis)


def on_device(transition, emission, token_ids, forward, backward_last):
    row_count = lax.axis_size("row")
    col_count = lax.axis_size("col")
    col_index = lax.axis_index("col")
    ratio = col_count // row_count
    local_seqs = forward.shape[1]
    block_src = transition.shape[0]
    block_dst = transition.shape[1]
    seq_total = local_seqs * col_count
    forward_all = lax.all_gather(forward, "col", axis=1, tiled=True)
    backward_next = lax.all_gather(backward_last, "row", axis=0, tiled=True)
    columns = lax.broadcasted_iota(jnp.int32, (seq_total, emission.shape[0]), 1)
    window = transition[:, :DW]
    totals = jnp.zeros((block_src, DW), jnp.float32)
    outputs = [None, None]
    for step in (1, 0):
        onehot = (token_ids[step][:, None] == columns).astype(jnp.bfloat16)
        emitted = jnp.dot(onehot, emission, preferred_element_type=jnp.float32)
        weighted_back = (emitted * backward_next).astype(jnp.bfloat16)
        partial_value = lax.dot_general(
            weighted_back, transition, (((1,), (1,)), ((), ())), preferred_element_type=jnp.float32
        )
        alpha_all = forward_all[step].astype(jnp.float32)
        summed = lax.psum(partial_value, "col")
        mine = lax.dynamic_slice_in_dim(summed, col_index * local_seqs, local_seqs, 0)
        alpha_mine = forward[step].astype(jnp.float32)
        local_norm = lax.psum(jnp.sum(alpha_mine * mine, axis=1), "row")
        normal_all = lax.all_gather(local_norm, "col", axis=0, tiled=True)
        normal_mine = lax.dynamic_slice_in_dim(normal_all, col_index * local_seqs, local_seqs, 0)
        outputs[step] = mine / normal_mine[:, None]
        scaled = (alpha_all / normal_all[:, None]).astype(jnp.bfloat16)
        totals = totals + lax.dot_general(
            scaled,
            weighted_back[:, :DW],
            (((0,), (0,)), ((), ())),
            preferred_element_type=jnp.float32,
        )
        if step == 1:
            whole = summed / normal_all[:, None]
            piece = lax.dynamic_slice_in_dim(whole, col_index % ratio * block_dst, block_dst, 1)
            backward_next = spread(piece, "row", col_index // ratio)
    counts = window.astype(jnp.float32) * totals * (H * H / N)
    return (jnp.stack(outputs), counts)


def solution(mesh):
    in_specs = (P("row", "col"), P(None, "col"), P(), P(None, "col", "row"), P("row", "col"))
    out_specs = (P(None, "col", "row"), P("row", "col"))
    return jax.shard_map(
        on_device, mesh=mesh, in_specs=in_specs, out_specs=out_specs, check_vma=False
    )
```

profile of v0, /device:TPU:0, one launch (start us, length us, event | category | flops | bytes accessed | tf_op | source)
XLA Modules:
  0.0 741.6 jit_solution(9007567216397277755)
XLA Ops:
  7.2 0.0 copy-start
  7.2 0.0 all-gather.3.cloned.1.call-start
  7.2 0.7 all-gather.3.cloned.1.call-update
  7.9 0.0 all-reduce.6.cloned.1.call-start
  8.0 0.8 fusion.17
  8.7 32.1 %all-gather.3.cloned.1.call-done = f32[192,4096]{1,0:T(8,128)} async-done(((f32[48,4096]{1,0:T(8,128)}), f32[192,4096]{1,0:T(8,128)}) %all-gather.3.cloned.1.call-update) | async-done | bytes 3145744 | tf_op jit(solution)/shard_map/all_gather | solution.py:26
  40.8 0.0 copy-done
  40.8 2.5 fusion.5
  43.3 31.1 %fusion.18 = f32[192,8192]{1,0:T(8,128)} fusion(bf16[192,4096]{1,0:T(8,128)(2,1)S(1)} %fusion.5, bf16[8192,4096]{1,0:T(8,128)(2,1)} %param.5), kind=kOutput, calls=%fused_computation.31 | convolution fusion | flops 12884901888 | bytes 74973184 | tf_op jit(solution)/shard_map/dot_general | solution.py:35
  74.5 0.0 copy-start.3
  74.5 0.0 copy-start.1
  74.5 0.0 all-reduce.6.cloned.1.call-update
  74.5 0.0 all-reduce.8.cloned.1.call-start
  74.6 0.6 copy-done.3
  75.1 0.6 dynamic-slice
  76.4 209.8 %all-reduce.6.cloned.1.call-done = f32[192,8192]{1,0:T(8,128)} async-done(((f32[192,8192]{1,0:T(8,128)}), f32[192,8192]{1,0:T(8,128)}) %all-reduce.6.cloned.1.call-update) | async-done | bytes 6291472 | tf_op jit(solution)/shard_map/psum | solution.py:39
  286.2 0.0 copy-done.1
  286.2 1.3 fusion.12
  287.5 6.9 psum.36
  294.4 0.2 dynamic-update-slice
  294.7 19.4 %all-reduce = f32[192]{0:T(256)S(1)} all-reduce(f32[192]{0:T(256)S(1)} %dynamic-update-slice), channel_id=1, replica_groups=mesh['row'=4,'col'=8] {'col'}, use_global_device_ids=true, to_apply=%add | all-reduce | flops 192 | bytes 1536
  314.1 4.0 fusion.7
  318.1 0.0 all-reduce.8.cloned.1.call-update
  318.1 0.0 all-gather.5.cloned.1.call-start
  318.1 0.5 all-gather.5.cloned.1.call-update
  318.7 0.0 all-reduce.10.cloned.1.call-start
  318.7 64.3 %all-reduce.8.cloned.1.call-done = f32[192,4096]{1,0:T(8,128)} async-done(((f32[192,4096]{1,0:T(8,128)}), f32[192,4096]{1,0:T(8,128)}) %all-reduce.8.cloned.1.call-update) | async-done | bytes 3145744 | tf_op jit(solution)/shard_map/psum | solution.py:13
  383.0 3.7 fusion.4
  386.7 30.8 %fusion.19 = f32[192,8192]{1,0:T(8,128)} fusion(bf16[192,4096]{1,0:T(8,128)(2,1)} %fusion.4, bf16[8192,4096]{1,0:T(8,128)(2,1)} %param.5), kind=kOutput, calls=%fused_computation.32 | convolution fusion | flops 12884901888 | bytes 74973184 | tf_op jit(solution)/shard_map/dot_general | solution.py:35
  417.5 0.0 all-reduce.10.cloned.1.call-update
  417.5 0.1 dynamic_slice.19
  417.6 0.0 copy-start.2
  417.6 66.8 %all-gather.5.cloned.1.call-done = bf16[2,192,8192]{2,1,0:T(8,128)(2,1)} async-done(((bf16[2,24,8192]{2,1,0:T(8,128)(2,1)}), bf16[2,192,8192]{2,1,0:T(8,128)(2,1)}) %all-gather.5.cloned.1.call-update) | async-done | bytes 6291472 | tf_op jit(solution)/shard_map/all_gather | solution.py:25
  484.4 5.4 fusion.9
  489.9 1.3 divide_bitcast_fusion
  491.1 207.2 %all-reduce.10.cloned.1.call-done = f32[192,8192]{1,0:T(8,128)} async-done(((f32[192,8192]{1,0:T(8,128)}), f32[192,8192]{1,0:T(8,128)}) %all-reduce.10.cloned.1.call-update) | async-done | bytes 6291472 | tf_op jit(solution)/shard_map/psum | solution.py:39
  698.3 0.0 copy-done.2
  698.3 1.3 fusion.11
  699.6 6.9 psum.39
  706.5 0.2 dynamic-update-slice.1
  706.7 19.4 %all-reduce.1 = f32[192]{0:T(256)S(1)} all-reduce(f32[192]{0:T(256)S(1)} %dynamic-update-slice.1), channel_id=1, replica_groups=mesh['row'=4,'col'=8] {'col'}, use_global_device_ids=true, to_apply=%add.1 | all-reduce | flops 192 | bytes 1536
  726.1 0.0 copy-start.4
  726.2 0.1 dynamic_slice.18
  726.2 1.4 divide_bitcast_fusion.1
  727.6 1.2 pad_maximum_fusion
  728.9 0.0 copy-done.4
  728.9 6.2 fusion.1
  (2 shorter events, 0.0 us)
Async XLA Ops:
  7.2 33.7 %copy-start = (bf16[96,4096]{1,0:T(8,128)(2,1)S(1)}, bf16[96,4096]{1,0:T(8,128)(2,1)}, u32[]{:S(2)}) copy-start(bf16[96,4096]{1,0:T(8,128)(2,1)} %param.6) | copy-start | bytes 2359300
  7.2 33.7 %all-gather.3.cloned.1.call-start = ((), (), s32[]{:S(2)}) async-start(), calls=%async_computation | async-start | bytes 3932160 | tf_op jit(solution)/shard_map/all_gather | solution.py:26
  7.9 278.3 %all-reduce.6.cloned.1.call-start = ((), (), s32[]{:S(2)}) async-start(), calls=%async_computation.1 | async-start | bytes 12582912 | tf_op jit(solution)/shard_map/psum | solution.py:39
  74.5 0.7 copy-start.3
  74.5 211.8 %copy-start.1 = (bf16[2,24,8192]{2,1,0:T(8,128)(2,1)S(1)}, bf16[2,24,8192]{2,1,0:T(8,128)(2,1)}, u32[]{:S(2)}) copy-start(bf16[2,24,8192]{2,1,0:T(8,128)(2,1)} %param.8) | copy-start | bytes 2359300
  74.5 308.5 %all-reduce.8.cloned.1.call-start = ((), (), s32[]{:S(2)}) async-start(), calls=%async_computation.2 | async-start | bytes 6291456 | tf_op jit(solution)/shard_map/psum | solution.py:13
  318.1 166.4 %all-gather.5.cloned.1.call-start = ((), (), s32[]{:S(2)}) async-start(), calls=%async_computation.4 | async-start | bytes 7077888 | tf_op jit(solution)/shard_map/all_gather | solution.py:25
  318.7 379.7 %all-reduce.10.cloned.1.call-start = ((), (), s32[]{:S(2)}) async-start(), calls=%async_computation.3 | async-start | bytes 12582912 | tf_op jit(solution)/shard_map/psum | solution.py:39
  417.6 280.7 %copy-start.2 = (bf16[2,24,8192]{2,1,0:T(8,128)(2,1)S(1)}, bf16[2,24,8192]{2,1,0:T(8,128)(2,1)}, u32[]{:S(2)}) copy-start(bf16[2,24,8192]{2,1,0:T(8,128)(2,1)} %param.8) | copy-start | bytes 2359300
  726.1 2.7 copy-start.4
Sparse Core Ops, SparseCore 0:
  9.6 31.2 all-gather.2
  74.6 211.5 all-reduce.5
  318.2 64.7 all-reduce.7
  385.3 99.1 all-gather.4
  488.5 209.7 all-reduce.9
where the time goes:
time: 742 us
  waiting for transfers between devices  582 us (78%)
  matrix products  79.7 us (11%)
  blocking collectives  52.5 us (7%)
  between operations  14.5 us (2%)
  other arithmetic  10.5 us (1%)
    psum x2, waiting for transfers between devices, on_device(): summed = lax.psum(partial_value, 'col')  417 us
    all_gather x1, waiting for transfers between devices, on_device(): forward_all = lax.all_gather(forward, 'col', axis=1, tiled=True)  66.8 us
    psum x1, waiting for transfers between devices, spread(): return lax.psum(kept, axis)  64.3 us
    dot_general x2, matrix products, on_device(): lax.dot_general(weighted_back, transition, (((1,), (1,)), ((), ())), pref...  61.9 us
    unnamed x2, blocking collectives  38.8 us
    all_gather x1, waiting for transfers between devices, on_device(): backward_next = lax.all_gather(backward_last, 'row', axis=0, tiled=True)  32.1 us
  transfers between devices with their start and end apart: 5, of which 5 were waited for; matrix products, arithmetic and copies ran while one was open for 6% of the time, Pallas kernels for 0%

commit v1 on v0

--- a/solution.py
+++ b/solution.py
@@ -36,7 +36,8 @@
             weighted_back, transition, (((1,), (1,)), ((), ())), preferred_element_type=jnp.float32
         )
         alpha_all = forward_all[step].astype(jnp.float32)
-        summed = lax.psum(partial_value, "col")
+        parts = lax.all_gather(partial_value, "col", axis=0, tiled=False)
+        summed = parts.sum(axis=0)
         mine = lax.dynamic_slice_in_dim(summed, col_index * local_seqs, local_seqs, 0)
         alpha_mine = forward[step].astype(jnp.float32)
         local_norm = lax.psum(jnp.sum(alpha_mine * mine, axis=1), "row")

time: 742 us -> 2260 us (3.05)
  waiting for transfers between devices: 582 us -> 2060 us
  other arithmetic: 10.5 us -> 50.7 us
    all_gather x0 -> x2, waiting for transfers between devices: none -> 1900 us  [on_device(): parts = lax.all_gather(partial_value, 'col', axis=0, tiled=False)]
    psum x2 -> x0, waiting for transfers between devices: 417 us -> none  [on_device(): summed = lax.psum(partial_value, 'col')]
    reduce_sum x0 -> x2, other arithmetic: none -> 40.1 us  [on_device(): summed = parts.sum(axis=0)]
  transfers between devices with their start and end apart: 5 -> 5, of which waited for: 5 -> 5; matrix products, arithmetic and copies ran while one was open for 6% -> 2% of each run, Pallas kernels for 0% -> 0%
where the time goes in v1:
time: 2260 us
  waiting for transfers between devices  2060 us (91%)
  matrix products  79.7 us (4%)
  blocking collectives  54.5 us (2%)
  other arithmetic  50.7 us (2%)
    all_gather x2, waiting for transfers between devices, on_device(): parts = lax.all_gather(partial_value, 'col', axis=0, tiled=False)  1900 us
    all_gather x1, waiting for transfers between devices, on_device(): forward_all = lax.all_gather(forward, 'col', axis=1, tiled=True)  66.7 us
    psum x1, waiting for transfers between devices, spread(): return lax.psum(kept, axis)  64.1 us
    dot_general x2, matrix products, on_device(): lax.dot_general(weighted_back, transition, (((1,), (1,)), ((), ())), pref...  61.9 us
  transfers between devices with their start and end apart: 5, of which 5 were waited for; matrix products, arithmetic and copies ran while one was open for 2% of the time, Pallas kernels for 0%

profile of v1, /device:TPU:0, one launch (start us, length us, event | category | flops | bytes accessed | tf_op | source)
XLA Modules:
  0.0 2262.0 jit_solution(6924776727963058960)
XLA Ops:
  7.2 0.0 copy-start
  7.2 0.0 all-gather.7.cloned.1.call-start
  7.2 0.7 all-gather.7.cloned.1.call-update
  7.9 0.0 all-gather.11.cloned.1.call-start
  8.0 0.8 fusion.17
  8.7 32.1 %all-gather.7.cloned.1.call-done = f32[192,4096]{1,0:T(8,128)} async-done(((f32[48,4096]{1,0:T(8,128)}), f32[192,4096]{1,0:T(8,128)}) %all-gather.7.cloned.1.call-update) | async-done | bytes 3145744 | tf_op jit(solution)/shard_map/all_gather | solution.py:26
  40.8 0.0 copy-done
  40.8 2.5 fusion.5
  43.3 31.1 %fusion.18 = f32[192,8192]{1,0:T(8,128)} fusion(bf16[192,4096]{1,0:T(8,128)(2,1)S(1)} %fusion.5, bf16[8192,4096]{1,0:T(8,128)(2,1)} %param.5), kind=kOutput, calls=%fused_computation.31 | convolution fusion | flops 12884901888 | bytes 74973184 | tf_op jit(solution)/shard_map/dot_general | solution.py:35
  74.4 0.0 copy-start.4
  74.4 0.0 all-gather.11.cloned.1.call-update
  74.5 0.0 all-reduce.4.cloned.1.call-start
  74.5 0.6 copy-done.4
  75.1 0.6 dynamic-slice
  76.3 950.6 %all-gather.11.cloned.1.call-done = f32[1536,8192]{1,0:T(8,128)} async-done(((f32[192,8192]{1,0:T(8,128)}), f32[1536,8192]{1,0:T(8,128)}) %all-gather.11.cloned.1.call-update) | async-done | bytes 50331664 | tf_op jit(solution)/shard_map/all_gather | solution.py:39
  1026.9 0.0 copy-start.2
  1026.9 20.0 reduce_sum.36
  1047.0 0.0 copy-done.2
  1047.0 1.3 fusion.12
  1048.3 6.9 psum.21
  1055.2 0.2 dynamic-update-slice
  1055.4 20.4 all-reduce
  1075.8 4.0 fusion.7
  1079.8 0.0 all-reduce.4.cloned.1.call-update
  1079.8 0.0 all-gather.9.cloned.1.call-start
  1079.8 0.5 all-gather.9.cloned.1.call-update
  1080.4 0.0 all-gather.13.cloned.1.call-start
  1080.4 64.1 %all-reduce.4.cloned.1.call-done = f32[192,4096]{1,0:T(8,128)} async-done(((f32[192,4096]{1,0:T(8,128)}), f32[192,4096]{1,0:T(8,128)}) %all-reduce.4.cloned.1.call-update) | async-done | bytes 3145744 | tf_op jit(solution)/shard_map/psum | solution.py:13
  1144.5 3.6 fusion.4
  1148.2 30.8 %fusion.19 = f32[192,8192]{1,0:T(8,128)} fusion(bf16[192,4096]{1,0:T(8,128)(2,1)} %fusion.4, bf16[8192,4096]{1,0:T(8,128)(2,1)} %param.5), kind=kOutput, calls=%fused_computation.32 | convolution fusion | flops 12884901888 | bytes 74973184 | tf_op jit(solution)/shard_map/dot_general | solution.py:35
  1179.0 0.0 all-gather.13.cloned.1.call-update
  1179.0 0.1 dynamic_slice.19
  1179.1 66.7 %all-gather.9.cloned.1.call-done = bf16[2,192,8192]{2,1,0:T(8,128)(2,1)} async-done(((bf16[2,24,8192]{2,1,0:T(8,128)(2,1)}), bf16[2,192,8192]{2,1,0:T(8,128)(2,1)}) %all-gather.9.cloned.1.call-update) | async-done | bytes 6291472 | tf_op jit(solution)/shard_map/all_gather | solution.py:25
  1245.8 5.4 fusion.9
  1251.2 1.3 divide_bitcast_fusion
  1252.5 945.2 %all-gather.13.cloned.1.call-done = f32[1536,8192]{1,0:T(8,128)} async-done(((f32[192,8192]{1,0:T(8,128)}), f32[1536,8192]{1,0:T(8,128)}) %all-gather.13.cloned.1.call-update) | async-done | bytes 50331664 | tf_op jit(solution)/shard_map/all_gather | solution.py:39
  2197.7 0.0 copy-start.3
  2197.7 20.0 reduce_sum.38
  2217.7 0.0 copy-done.3
  2217.7 1.3 fusion.11
  2219.0 6.9 psum.23
  2225.9 0.2 dynamic-update-slice.1
  2226.2 20.4 all-reduce.1
  2246.5 0.0 copy-start.5
  2246.5 0.1 dynamic_slice.18
  2246.6 1.4 divide_bitcast_fusion.1
  2248.0 1.2 pad_maximum_fusion
  2249.3 0.0 copy-done.5
  2249.3 0.0 copy-start.1
  2249.3 6.2 fusion.1
  2255.5 0.0 copy-done.1
  (2 shorter events, 0.0 us)
Async XLA Ops:
  7.2 33.7 %copy-start = (bf16[96,4096]{1,0:T(8,128)(2,1)S(1)}, bf16[96,4096]{1,0:T(8,128)(2,1)}, u32[]{:S(2)}) copy-start(bf16[96,4096]{1,0:T(8,128)(2,1)} %param.6) | copy-start | bytes 2359300
  7.2 33.7 %all-gather.7.cloned.1.call-start = ((), (), s32[]{:S(2)}) async-start(), calls=%async_computation | async-start | bytes 3932160 | tf_op jit(solution)/shard_map/all_gather | solution.py:26
  7.9 1019.0 %all-gather.11.cloned.1.call-start = ((), (), s32[]{:S(2)}) async-start(), calls=%async_computation.3 | async-start | bytes 56623104 | tf_op jit(solution)/shard_map/all_gather | solution.py:39
  74.4 0.7 copy-start.4
  74.5 1070.1 %all-reduce.4.cloned.1.call-start = ((), (), s32[]{:S(2)}) async-start(), calls=%async_computation.1 | async-start | bytes 6291456 | tf_op jit(solution)/shard_map/psum | solution.py:13
  1026.9 20.1 copy-start.2
  1079.8 166.0 %all-gather.9.cloned.1.call-start = ((), (), s32[]{:S(2)}) async-start(), calls=%async_computation.2 | async-start | bytes 7077888 | tf_op jit(solution)/shard_map/all_gather | solution.py:25
  1080.4 1117.3 %all-gather.13.cloned.1.call-start = ((), (), s32[]{:S(2)}) async-start(), calls=%async_computation.4 | async-start | bytes 56623104 | tf_op jit(solution)/shard_map/all_gather | solution.py:39
  2197.7 20.1 copy-start.3
  2246.5 2.7 copy-start.5
  2249.3 6.3 copy-start.1
Sparse Core Ops, SparseCore 0:
  9.6 31.2 all-gather.6
  74.6 952.3 all-gather.10
  1079.9 64.5 all-reduce.3
  1146.6 99.1 all-gather.8
  1247.1 950.4 all-gather.12
